TPU v7x, 32 devices: a whole 2x2x4 slice. The times are simulated.
32 devices in a mesh: ctx: 16 (over z, x, core), head: 2 (over y).
Axes of the slice: x: 2, y: 2, z: 4, core: 2. Of those that a mesh axis runs over, the one named last changes fastest.
Arguments:
- queries: bfloat16 [4096, 16, 128], P(('ctx', 'head')), may hold values from -8 to 8
- keys: bfloat16 [4096, 16, 128], P(('ctx', 'head')), may hold values from -6 to 6
- values: bfloat16 [4096, 16, 128], P(('ctx', 'head')), may hold values from -6 to 6
- out_grad: bfloat16 [4096, 16, 128], P(('ctx', 'head')), may hold values from -6 to 6
- block_lists: int32 [16, 3], P('ctx'), may hold values from 0 to 15, as said below
Outputs:
- attended: bfloat16 [4096, 16, 128], P(('ctx', 'head'))
- grad_query: bfloat16 [4096, 16, 128], P(('ctx', 'head'))
- grad_key: bfloat16 [4096, 16, 128], P(('ctx', 'head'))
- grad_value: bfloat16 [4096, 16, 128], P(('ctx', 'head'))
Inputs may be any that keep to these rules, and one draw needn't show every extreme that they name: `block_lists`: row b begins with b; its other entries are distinct blocks among b - 3 to b - 1, as many of them as exist up to 2, and b again where fewer exist.
All inputs are finite; a program needn't handle non-finite values.
Results may differ from a plain program's by a relative error of at most 0.015.
Values may be sent and summed in bfloat16 or wider, within the bound.
A program may use at most 64 MiB of HBM per device.

v0:
```python
import math
import jax
import jax.numpy as jnp
from jax import lax
from jax.sharding import PartitionSpec as P

R = 3


def from_behind(block, axis, distance):
    devices = range(lax.axis_size(axis))
    route = [(i - distance, i) for i in devices if i - distance in devices]
    return lax.ppermute(block, axis, route)


def attend(query_rows, key_window, value_window, grad_rows, allowed):
    score_scale = 1.0 / math.sqrt(query_rows.shape[-1])
    scores = (
        jnp.einsum("thd,shd->hts", query_rows, key_window, preferred_element_type=jnp.float32)
        * score_scale
    )
    scores = jnp.where(allowed[None], scores, -jnp.inf)
    highest = jnp.max(scores, axis=2, keepdims=True)
    weights = jnp.exp(scores - highest)
    probability = weights / jnp.sum(weights, axis=2, keepdims=True)
    probs_low = probability.astype(jnp.bfloat16)
    attended = jnp.einsum(
        "hts,shd->thd", probs_low, value_window, preferred_element_type=jnp.float32
    ).astype(jnp.bfloat16)
    grad_probs = jnp.einsum(
        "thd,shd->hts", grad_rows, value_window, preferred_element_type=jnp.float32
    )
    centre = jnp.sum(grad_rows.astype(jnp.float32) * attended.astype(jnp.float32), axis=2).T[
        :, :, None
    ]
    grad_scores = (probability * (grad_probs - centre)).astype(jnp.bfloat16)
    grad_query = (
        jnp.einsum("hts,shd->thd", grad_scores, key_window, preferred_element_type=jnp.float32)
        * score_scale
    ).astype(jnp.bfloat16)
    key_terms = (
        jnp.einsum("hts,thd->shd", grad_scores, query_rows, preferred_element_type=jnp.float32)
        * score_scale
    )
    value_terms = jnp.einsum(
        "hts,thd->shd", probs_low, grad_rows, preferred_element_type=jnp.float32
    )
    return (attended, grad_query, key_terms, value_terms)


def block_mask(block_permitted, tile_lower_mask, length):
    row_ids = jnp.arange(length)
    lower_tri = row_ids[:, None] >= row_ids[None, :]
    allowed = block_permitted[None, :, None] & (
        (~tile_lower_mask)[None, :, None] | lower_tri[:, None, :]
    )
    return allowed.reshape(length, block_permitted.shape[0] * length)


def local(queries, keys, values, out_grad, block_lists):
    query_rows, key_rows, value_rows, grad_rows = (
        lax.all_to_all(queries, "head", split_axis=1, concat_axis=0, tiled=True),
        lax.all_to_all(keys, "head", split_axis=1, concat_axis=0, tiled=True),
        lax.all_to_all(values, "head", split_axis=1, concat_axis=0, tiled=True),
        lax.all_to_all(out_grad, "head", split_axis=1, concat_axis=0, tiled=True),
    )
    length = query_rows.shape[0]
    head_count = query_rows.shape[1]
    width = query_rows.shape[2]
    position = lax.axis_index("ctx")
    listing = block_lists[0]
    key_tiles = [key_rows]
    value_tiles = [value_rows]
    held_key, held_value = (key_rows, value_rows)
    for distance in range(1, R + 1):
        held_key, held_value = from_behind((held_key, held_value), "ctx", 1)
        key_tiles.append(held_key)
        value_tiles.append(held_value)
    offsets = jnp.arange(R + 1, dtype=jnp.int32)
    candidate_block = position - offsets
    block_permitted = jnp.any(candidate_block[:, None] == listing[None, :], axis=1) & (
        candidate_block >= 0
    )
    tile_lower_mask = offsets == 0
    key_window = jnp.concatenate(key_tiles, axis=0)
    value_window = jnp.concatenate(value_tiles, axis=0)
    count = key_window.shape[0] // length
    allowed = block_mask(block_permitted, tile_lower_mask, length)
    attended, grad_query, key_terms, value_terms = attend(
        query_rows, key_window, value_window, grad_rows, allowed
    )
    key_terms = key_terms.reshape(count, length, head_count, width)
    value_terms = value_terms.reshape(count, length, head_count, width)
    key_total = key_terms[0]
    value_total = value_terms[0]
    for distance in range(1, R + 1):
        back_key, back_value = from_behind(
            (key_terms[distance].astype(jnp.bfloat16), value_terms[distance].astype(jnp.bfloat16)),
            "ctx",
            -distance,
        )
        key_total = key_total + back_key.astype(jnp.float32)
        value_total = value_total + back_value.astype(jnp.float32)
    return (
        lax.all_to_all(attended, "head", split_axis=0, concat_axis=1, tiled=True),
        lax.all_to_all(grad_query, "head", split_axis=0, concat_axis=1, tiled=True),
        lax.all_to_all(
            key_total.astype(jnp.bfloat16), "head", split_axis=0, concat_axis=1, tiled=True
        ),
        lax.all_to_all(
            value_total.astype(jnp.bfloat16), "head", split_axis=0, concat_axis=1, tiled=True
        ),
    )


def solution(mesh):
    placed = (
        P(("ctx", "head"), None, None),
        P(("ctx", "head"), None, None),
        P(("ctx", "head"), None, None),
        P(("ctx", "head"), None, None),
        P("ctx", None),
    )
    return jax.shard_map(
        local,
        mesh=mesh,
        in_specs=placed,
        out_specs=(
            P(("ctx", "head"), None, None),
            P(("ctx", "head"), None, None),
            P(("ctx", "head"), None, None),
            P(("ctx", "head"), None, None),
        ),
        check_vma=False,
    )
```

profile of v0, /device:TPU:10, one launch (start us, length us, event | category | flops | bytes accessed | tf_op | source)
XLA Modules:
  0.0 160.8 jit_solution(1103698851266385415)
XLA Ops:
  1.9 10.8 %all_to_all.144 = bf16[128,16,128]{2,0,1:T(8,128)(2,1)S(1)} all-to-all(bf16[128,16,128]{2,0,1:T(8,128)(2,1)S(1)} %copy.47), channel_id=1, replica_groups=mesh['ctx'=16,'head'=2] {'head'}, dimensions={1} | all-to-all | bytes 1048576 | tf_op jit(solution)/shard_map/all_to_all | solution.py:63
  15.9 11.2 %all_to_all.145 = bf16[128,16,128]{2,0,1:T(8,128)(2,1)S(1)} all-to-all(bf16[128,16,128]{2,0,1:T(8,128)(2,1)S(1)} %copy.45), channel_id=1, replica_groups=mesh['ctx'=16,'head'=2] {'head'}, dimensions={1} | all-to-all | bytes 1048576 | tf_op jit(solution)/shard_map/all_to_all | solution.py:64
  27.8 2.4 %collective-permute-start = (bf16[256,8,128]{0,2,1:T(8,128)(2,1)S(1)}, bf16[256,8,128]{0,2,1:T(8,128)(2,1)}, u32[]{:S(2)}, u32[]{:S(2)}) collective-permute-start(bf16[256,8,128]{0,2,1:T(8,128)(2,1)S(1)} %all_to_all.107), channel_id=1, source_target_pairs={{0,2},{2,4},{4,6},{6,8},{8,10},{10,12},{12,14},{14,16},{16,18},{18... | collective-permute-start | bytes 1572872 | tf_op jit(solution)/shard_map/ppermute | solution.py:13
  30.2 3.2 %collective-permute-start.4 = (bf16[256,8,128]{2,0,1:T(8,128)(2,1)}, bf16[256,8,128]{2,0,1:T(8,128)(2,1)}, u32[]{:S(2)}, u32[]{:S(2)}) collective-permute-start(bf16[256,8,128]{2,0,1:T(8,128)(2,1)} %collective-permute-done.3), channel_id=1, source_target_pairs={{0,2},{2,4},{4,6},{6,8},{8,10},{10,12},{12,14},{14,16},{16,18},{18... | collective-permute-start | bytes 1572872 | tf_op jit(solution)/shard_map/ppermute | solution.py:13
  34.3 3.5 %all-to-all-start.2 = ((bf16[128,16,128]{2,0,1:T(8,128)(2,1)}), bf16[128,16,128]{2,0,1:T(8,128)(2,1)S(1)}, u32[]{:S(2)}, u32[]{:S(2)}) async-start(bf16[128,16,128]{2,0,1:T(8,128)(2,1)} %copy.49), calls=%async_computation.2 | async-start | bytes 1048576 | tf_op jit(solution)/shard_map/all_to_all | solution.py:62
  38.9 2.3 %collective-permute-start.1 = (bf16[256,8,128]{0,2,1:T(8,128)(2,1)}, bf16[256,8,128]{0,2,1:T(8,128)(2,1)}, u32[]{:S(2)}, u32[]{:S(2)}) collective-permute-start(bf16[256,8,128]{0,2,1:T(8,128)(2,1)} %collective-permute-done), channel_id=1, source_target_pairs={{0,2},{2,4},{4,6},{6,8},{8,10},{10,12},{12,14},{14,16},{16,18},{18... | collective-permute-start | bytes 1572872 | tf_op jit(solution)/shard_map/ppermute | solution.py:13
  41.2 5.3 %all-to-all-done.2 = bf16[128,16,128]{2,0,1:T(8,128)(2,1)S(1)} async-done(((bf16[128,16,128]{2,0,1:T(8,128)(2,1)}), bf16[128,16,128]{2,0,1:T(8,128)(2,1)S(1)}, u32[]{:S(2)}, u32[]{:S(2)}) %all-to-all-start.2) | async-done | bytes 524320 | tf_op jit(solution)/shard_map/all_to_all | solution.py:62
  46.6 3.5 %all-to-all-start.4 = ((bf16[128,16,128]{2,0,1:T(8,128)(2,1)}), bf16[128,16,128]{2,0,1:T(8,128)(2,1)S(1)}, u32[]{:S(2)}, u32[]{:S(2)}) async-start(bf16[128,16,128]{2,0,1:T(8,128)(2,1)} %copy.54), calls=%async_computation.4 | async-start | bytes 1048576 | tf_op jit(solution)/shard_map/all_to_all | solution.py:65
  53.4 4.7 %all-to-all-done.4 = bf16[128,16,128]{2,0,1:T(8,128)(2,1)S(1)} async-done(((bf16[128,16,128]{2,0,1:T(8,128)(2,1)}), bf16[128,16,128]{2,0,1:T(8,128)(2,1)S(1)}, u32[]{:S(2)}, u32[]{:S(2)}) %all-to-all-start.4) | async-done | bytes 524320 | tf_op jit(solution)/shard_map/all_to_all | solution.py:65
  63.1 7.6 %fusion.23 = (f32[8,256]{1,0:T(8,128)S(1)}, f32[8,256,1024]{1,2,0:T(8,128)}) fusion(pred[256,1024]{0,1:T(8,128)(4,1)S(1)} %fusion.16, bf16[256,8,128]{2,0,1:T(8,128)(2,1)} %bitcast.92, bf16[256,8,128]{2,0,1:T(8,128)(2,1)} %collective-permute-done.5, bf16[256,8,128]{2,0,1:T(8,128)(2,1)} %collective-permute-done.4, ...), kind=kOutput, calls=%fused_computation.48 | convolution fusion | flops 553649152 | bytes 11280384 | tf_op jit(solution)/shard_map/sub | solution.py:24
  70.7 4.3 %fusion.6 = bf16[8,256,1024]{1,2,0:T(8,128)(2,1)S(1)} fusion(f32[8,256,1024]{1,2,0:T(8,128)} %get-tuple-element.11, f32[8,256]{1,0:T(8,128)S(1)} %get-tuple-element.10), kind=kLoop, calls=%fused_computation.11 | loop fusion | flops 4194304 | bytes 12591104 | tf_op jit(solution)/shard_map/convert_element_type | solution.py:26
  78.3 3.2 %fusion.24 = (bf16[1024,8,128]{2,0,1:T(8,128)(2,1)S(1)}, f32[1024,8,128]{2,0,1:T(8,128)}) fusion(bf16[8,256,1024]{1,2,0:T(8,128)(2,1)S(1)} %fusion.1, bf16[256,8,128]{2,0,1:T(8,128)(2,1)S(1)} %bitcast.93), kind=kOutput, calls=%fused_computation.49 | convolution fusion | flops 538968064 | bytes 11010048 | tf_op jit(solution)/shard_map/hts,thd->shd/dot_general | solution.py:42
  82.7 3.6 %collective-permute-start.6 = (bf16[256,8,128]{2,0,1:T(8,128)(2,1)}, bf16[256,8,128]{2,0,1:T(8,128)(2,1)}, u32[]{:S(2)}, u32[]{:S(2)}) collective-permute-start(bf16[256,8,128]{2,0,1:T(8,128)(2,1)} %get-tuple-element.7), channel_id=1, source_target_pairs={{2,0},{4,2},{6,4},{8,6},{10,8},{12,10},{14,12},{16,14},{18,16},{20... | collective-permute-start | bytes 1572872 | tf_op jit(solution)/shard_map/ppermute | solution.py:13
  88.3 3.6 %collective-permute-start.7 = (bf16[256,8,128]{2,0,1:T(8,128)(2,1)}, bf16[256,8,128]{2,0,1:T(8,128)(2,1)}, u32[]{:S(2)}, u32[]{:S(2)}) collective-permute-start(bf16[256,8,128]{2,0,1:T(8,128)(2,1)} %get-tuple-element.9), channel_id=1, source_target_pairs={{4,0},{6,2},{8,4},{10,6},{12,8},{14,10},{16,12},{18,14},{20,16},{2... | collective-permute-start | bytes 1572872 | tf_op jit(solution)/shard_map/ppermute | solution.py:13
  91.9 3.1 %fusion.9 = bf16[256,8,128]{0,2,1:T(8,128)(2,1)} fusion(bf16[8,256,1024]{1,2,0:T(8,128)(2,1)S(1)} %fusion.1, bf16[256,8,128]{2,0,1:T(8,128)(2,1)} %collective-permute-done.5, bf16[256,8,128]{2,0,1:T(8,128)(2,1)} %collective-permute-done.4, bf16[256,8,128]{2,0,1:T(8,128)(2,1)} %collective-permute-done.3, bf16[256,8,128]{2,0,1:T(8,128)(2,1)S(1)} %bitcast.96), kind=kOutput, calls=%fused_computation.18 | convolution fusion | flops 545783808 | bytes 6815744 | tf_op jit(solution)/shard_map/hts,shd->thd/dot_general | solution.py:38
  95.0 3.3 %fusion.25 = (bf16[1024,8,128]{2,0,1:T(8,128)(2,1)S(1)}, f32[1024,8,128]{2,0,1:T(8,128)}) fusion(bf16[8,256,1024]{1,2,0:T(8,128)(2,1)S(1)} %fusion.6, bf16[256,8,128]{0,2,1:T(8,128)(2,1)S(1)} %all_to_all.123), kind=kOutput, calls=%fused_computation.50 | convolution fusion | flops 537919488 | bytes 11010048 | tf_op jit(solution)/shard_map/hts,thd->shd/dot_general | solution.py:45
  98.3 2.1 %copy.60 = bf16[256,8,128]{2,1,0:T(8,128)(2,1)} copy(bf16[256,8,128]{0,2,1:T(8,128)(2,1)} %fusion.9) | data formatting | bytes 1048576 | tf_op jit(solution)/shard_map/convert_element_type | solution.py:40
  100.4 3.5 %all-to-all-start.5 = ((bf16[256,8,128]{2,1,0:T(8,128)(2,1)}), bf16[256,8,128]{2,1,0:T(8,128)(2,1)S(1)}, u32[]{:S(2)}, u32[]{:S(2)}) async-start(bf16[256,8,128]{2,1,0:T(8,128)(2,1)} %copy.60), calls=%async_computation.5 | async-start | bytes 1048576 | tf_op jit(solution)/shard_map/all_to_all | solution.py:106
  112.6 3.5 %all-to-all-start.3 = ((bf16[256,8,128]{2,1,0:T(8,128)(2,1)}), bf16[256,8,128]{2,1,0:T(8,128)(2,1)S(1)}, u32[]{:S(2)}, u32[]{:S(2)}) async-start(bf16[256,8,128]{2,1,0:T(8,128)(2,1)} %copy.52), calls=%async_computation.3 | async-start | bytes 1048576 | tf_op jit(solution)/shard_map/all_to_all | solution.py:105
  116.1 6.5 %collective-permute-done.7 = bf16[256,8,128]{2,0,1:T(8,128)(2,1)} collective-permute-done((bf16[256,8,128]{2,0,1:T(8,128)(2,1)}, bf16[256,8,128]{2,0,1:T(8,128)(2,1)}, u32[]{:S(2)}, u32[]{:S(2)}) %collective-permute-start.7) | collective-permute-done | bytes 524320 | tf_op jit(solution)/shard_map/ppermute | solution.py:13
  125.7 3.5 %all-to-all-start.6 = ((bf16[256,8,128]{2,1,0:T(8,128)(2,1)}), bf16[256,8,128]{2,1,0:T(8,128)(2,1)S(1)}, u32[]{:S(2)}, u32[]{:S(2)}) async-start(bf16[256,8,128]{2,1,0:T(8,128)(2,1)} %copy.62), calls=%async_computation.6 | async-start | bytes 1048576 | tf_op jit(solution)/shard_map/all_to_all | solution.py:107
  129.2 17.7 %collective-permute-done.10 = bf16[256,8,128]{2,0,1:T(8,128)(2,1)} collective-permute-done((bf16[256,8,128]{2,0,1:T(8,128)(2,1)}, bf16[256,8,128]{2,0,1:T(8,128)(2,1)}, u32[]{:S(2)}, u32[]{:S(2)}) %collective-permute-start.10) | collective-permute-done | bytes 524320 | tf_op jit(solution)/shard_map/ppermute | solution.py:13
  149.8 3.5 %all-to-all-start.7 = ((bf16[256,8,128]{2,1,0:T(8,128)(2,1)}), bf16[256,8,128]{2,1,0:T(8,128)(2,1)S(1)}, u32[]{:S(2)}, u32[]{:S(2)}) async-start(bf16[256,8,128]{2,1,0:T(8,128)(2,1)} %copy.65), calls=%async_computation.7 | async-start | bytes 1048576 | tf_op jit(solution)/shard_map/all_to_all | solution.py:110
  156.0 3.9 %all-to-all-done.7 = bf16[256,8,128]{2,1,0:T(8,128)(2,1)S(1)} async-done(((bf16[256,8,128]{2,1,0:T(8,128)(2,1)}), bf16[256,8,128]{2,1,0:T(8,128)(2,1)S(1)}, u32[]{:S(2)}, u32[]{:S(2)}) %all-to-all-start.7) | async-done | bytes 524320 | tf_op jit(solution)/shard_map/all_to_all | solution.py:110
  (76 shorter events, 40.0 us)
Async XLA Ops:
  0.6 32.7 %copy-start.1 = (bf16[128,16,128]{2,1,0:T(8,128)(2,1)S(1)}, bf16[128,16,128]{2,1,0:T(8,128)(2,1)}, u32[]{:S(2)}) copy-start(bf16[128,16,128]{2,1,0:T(8,128)(2,1)} %param.5) | copy-start | bytes 1572868
  1.9 35.9 %copy-start.2 = (bf16[128,16,128]{2,1,0:T(8,128)(2,1)S(1)}, bf16[128,16,128]{2,1,0:T(8,128)(2,1)}, u32[]{:S(2)}) copy-start(bf16[128,16,128]{2,1,0:T(8,128)(2,1)} %param.8) | copy-start | bytes 1572868
  12.7 26.1 %copy-start.6 = (s32[1,3]{1,0:T(1,128)S(1)}, s32[1,3]{1,0:T(1,128)}, u32[]{:S(2)}) copy-start(s32[1,3]{1,0:T(1,128)} %param.9) | copy-start | bytes 40
  12.7 33.9 %copy-start.3 = (bf16[128,2,8,128]{3,0,1,2:T(8,128)(2,1)}, bf16[128,2,8,128]{3,0,1,2:T(8,128)(2,1)S(1)}, u32[]{:S(2)}) copy-start(bf16[128,2,8,128]{3,0,1,2:T(8,128)(2,1)S(1)} %copy.48) | copy-start | bytes 1572868
  12.7 17.4 %collective-permute-start.3 = (bf16[256,8,128]{2,0,1:T(8,128)(2,1)S(1)}, bf16[256,8,128]{2,0,1:T(8,128)(2,1)}, u32[]{:S(2)}, u32[]{:S(2)}) collective-permute-start(bf16[256,8,128]{2,0,1:T(8,128)(2,1)S(1)} %bitcast.94), channel_id=1, source_target_pairs={{0,2},{2,4},{4,6},{6,8},{8,10},{10,12},{12,14},{14,16},{16,18},{18... | collective-permute-start | bytes 1572872 | tf_op jit(solution)/shard_map/ppermute | solution.py:13
  27.8 11.2 %collective-permute-start = (bf16[256,8,128]{0,2,1:T(8,128)(2,1)S(1)}, bf16[256,8,128]{0,2,1:T(8,128)(2,1)}, u32[]{:S(2)}, u32[]{:S(2)}) collective-permute-start(bf16[256,8,128]{0,2,1:T(8,128)(2,1)S(1)} %all_to_all.107), channel_id=1, source_target_pairs={{0,2},{2,4},{4,6},{6,8},{8,10},{10,12},{12,14},{14,16},{16,18},{18... | collective-permute-start | bytes 1572872 | tf_op jit(solution)/shard_map/ppermute | solution.py:13
  30.2 19.9 %collective-permute-start.4 = (bf16[256,8,128]{2,0,1:T(8,128)(2,1)}, bf16[256,8,128]{2,0,1:T(8,128)(2,1)}, u32[]{:S(2)}, u32[]{:S(2)}) collective-permute-start(bf16[256,8,128]{2,0,1:T(8,128)(2,1)} %collective-permute-done.3), channel_id=1, source_target_pairs={{0,2},{2,4},{4,6},{6,8},{8,10},{10,12},{12,14},{14,16},{16,18},{18... | collective-permute-start | bytes 1572872 | tf_op jit(solution)/shard_map/ppermute | solution.py:13
  34.3 12.3 %all-to-all-start.2 = ((bf16[128,16,128]{2,0,1:T(8,128)(2,1)}), bf16[128,16,128]{2,0,1:T(8,128)(2,1)S(1)}, u32[]{:S(2)}, u32[]{:S(2)}) async-start(bf16[128,16,128]{2,0,1:T(8,128)(2,1)} %copy.49), calls=%async_computation.2 | async-start | bytes 1048576 | tf_op jit(solution)/shard_map/all_to_all | solution.py:62
  38.9 21.2 %collective-permute-start.1 = (bf16[256,8,128]{0,2,1:T(8,128)(2,1)}, bf16[256,8,128]{0,2,1:T(8,128)(2,1)}, u32[]{:S(2)}, u32[]{:S(2)}) collective-permute-start(bf16[256,8,128]{0,2,1:T(8,128)(2,1)} %collective-permute-done), channel_id=1, source_target_pairs={{0,2},{2,4},{4,6},{6,8},{8,10},{10,12},{12,14},{14,16},{16,18},{18... | collective-permute-start | bytes 1572872 | tf_op jit(solution)/shard_map/ppermute | solution.py:13
  46.6 11.6 %all-to-all-start.4 = ((bf16[128,16,128]{2,0,1:T(8,128)(2,1)}), bf16[128,16,128]{2,0,1:T(8,128)(2,1)S(1)}, u32[]{:S(2)}, u32[]{:S(2)}) async-start(bf16[128,16,128]{2,0,1:T(8,128)(2,1)} %copy.54), calls=%async_computation.4 | async-start | bytes 1048576 | tf_op jit(solution)/shard_map/all_to_all | solution.py:65
  50.1 13.0 %collective-permute-start.5 = (bf16[256,8,128]{2,0,1:T(8,128)(2,1)}, bf16[256,8,128]{2,0,1:T(8,128)(2,1)}, u32[]{:S(2)}, u32[]{:S(2)}) collective-permute-start(bf16[256,8,128]{2,0,1:T(8,128)(2,1)} %collective-permute-done.4), channel_id=1, source_target_pairs={{0,2},{2,4},{4,6},{6,8},{8,10},{10,12},{12,14},{14,16},{16,18},{18... | collective-permute-start | bytes 1572872 | tf_op jit(solution)/shard_map/ppermute | solution.py:13
  60.1 14.9 %collective-permute-start.2 = (bf16[256,8,128]{0,2,1:T(8,128)(2,1)}, bf16[256,8,128]{0,2,1:T(8,128)(2,1)S(1)}, u32[]{:S(2)}, u32[]{:S(2)}) collective-permute-start(bf16[256,8,128]{0,2,1:T(8,128)(2,1)} %collective-permute-done.1), channel_id=1, source_target_pairs={{0,2},{2,4},{4,6},{6,8},{8,10},{10,12},{12,14},{14,16},{16,18},{18... | collective-permute-start | bytes 1572872 | tf_op jit(solution)/shard_map/ppermute | solution.py:13
  78.3 13.6 %copy-start.4 = (bf16[128,2,8,128]{3,0,1,2:T(8,128)(2,1)S(1)}, bf16[128,2,8,128]{3,0,1,2:T(8,128)(2,1)}, u32[]{:S(2)}) copy-start(bf16[128,2,8,128]{3,0,1,2:T(8,128)(2,1)} %copy-done.3) | copy-start | bytes 1572868
  82.7 26.3 %collective-permute-start.6 = (bf16[256,8,128]{2,0,1:T(8,128)(2,1)}, bf16[256,8,128]{2,0,1:T(8,128)(2,1)}, u32[]{:S(2)}, u32[]{:S(2)}) collective-permute-start(bf16[256,8,128]{2,0,1:T(8,128)(2,1)} %get-tuple-element.7), channel_id=1, source_target_pairs={{2,0},{4,2},{6,4},{8,6},{10,8},{12,10},{14,12},{16,14},{18,16},{20... | collective-permute-start | bytes 1572872 | tf_op jit(solution)/shard_map/ppermute | solution.py:13
  86.4 29.7 %collective-permute-start.8 = (bf16[256,8,128]{2,0,1:T(8,128)(2,1)}, bf16[256,8,128]{2,0,1:T(8,128)(2,1)}, u32[]{:S(2)}, u32[]{:S(2)}) collective-permute-start(bf16[256,8,128]{2,0,1:T(8,128)(2,1)} %get-tuple-element.8), channel_id=1, source_target_pairs={{6,0},{8,2},{10,4},{12,6},{14,8},{16,10},{18,12},{20,14},{22,16},{... | collective-permute-start | bytes 1572872 | tf_op jit(solution)/shard_map/ppermute | solution.py:13
  88.3 34.2 %collective-permute-start.7 = (bf16[256,8,128]{2,0,1:T(8,128)(2,1)}, bf16[256,8,128]{2,0,1:T(8,128)(2,1)}, u32[]{:S(2)}, u32[]{:S(2)}) collective-permute-start(bf16[256,8,128]{2,0,1:T(8,128)(2,1)} %get-tuple-element.9), channel_id=1, source_target_pairs={{4,0},{6,2},{8,4},{10,6},{12,8},{14,10},{16,12},{18,14},{20,16},{2... | collective-permute-start | bytes 1572872 | tf_op jit(solution)/shard_map/ppermute | solution.py:13
  100.4 12.2 %all-to-all-start.5 = ((bf16[256,8,128]{2,1,0:T(8,128)(2,1)}), bf16[256,8,128]{2,1,0:T(8,128)(2,1)S(1)}, u32[]{:S(2)}, u32[]{:S(2)}) async-start(bf16[256,8,128]{2,1,0:T(8,128)(2,1)} %copy.60), calls=%async_computation.5 | async-start | bytes 1048576 | tf_op jit(solution)/shard_map/all_to_all | solution.py:106
  105.1 24.1 %collective-permute-start.9 = (bf16[256,8,128]{2,0,1:T(8,128)(2,1)}, bf16[256,8,128]{2,0,1:T(8,128)(2,1)S(1)}, u32[]{:S(2)}, u32[]{:S(2)}) collective-permute-start(bf16[256,8,128]{2,0,1:T(8,128)(2,1)} %get-tuple-element.4), channel_id=1, source_target_pairs={{2,0},{4,2},{6,4},{8,6},{10,8},{12,10},{14,12},{16,14},{18,16},{20... | collective-permute-start | bytes 1572872 | tf_op jit(solution)/shard_map/ppermute | solution.py:13
  107.1 22.0 %collective-permute-start.11 = (bf16[256,8,128]{2,0,1:T(8,128)(2,1)}, bf16[256,8,128]{2,0,1:T(8,128)(2,1)S(1)}, u32[]{:S(2)}, u32[]{:S(2)}) collective-permute-start(bf16[256,8,128]{2,0,1:T(8,128)(2,1)} %get-tuple-element.5), channel_id=1, source_target_pairs={{6,0},{8,2},{10,4},{12,6},{14,8},{16,10},{18,12},{20,14},{22,16},{... | collective-permute-start | bytes 1572872 | tf_op jit(solution)/shard_map/ppermute | solution.py:13
  109.1 37.8 %collective-permute-start.10 = (bf16[256,8,128]{2,0,1:T(8,128)(2,1)}, bf16[256,8,128]{2,0,1:T(8,128)(2,1)}, u32[]{:S(2)}, u32[]{:S(2)}) collective-permute-start(bf16[256,8,128]{2,0,1:T(8,128)(2,1)} %get-tuple-element.6), channel_id=1, source_target_pairs={{4,0},{6,2},{8,4},{10,6},{12,8},{14,10},{16,12},{18,14},{20,16},{2... | collective-permute-start | bytes 1572872 | tf_op jit(solution)/shard_map/ppermute | solution.py:13
  112.6 13.1 %all-to-all-start.3 = ((bf16[256,8,128]{2,1,0:T(8,128)(2,1)}), bf16[256,8,128]{2,1,0:T(8,128)(2,1)S(1)}, u32[]{:S(2)}, u32[]{:S(2)}) async-start(bf16[256,8,128]{2,1,0:T(8,128)(2,1)} %copy.52), calls=%async_computation.3 | async-start | bytes 1048576 | tf_op jit(solution)/shard_map/all_to_all | solution.py:105
  125.7 24.2 %all-to-all-start.6 = ((bf16[256,8,128]{2,1,0:T(8,128)(2,1)}), bf16[256,8,128]{2,1,0:T(8,128)(2,1)S(1)}, u32[]{:S(2)}, u32[]{:S(2)}) async-start(bf16[256,8,128]{2,1,0:T(8,128)(2,1)} %copy.62), calls=%async_computation.6 | async-start | bytes 1048576 | tf_op jit(solution)/shard_map/all_to_all | solution.py:107
  129.2 17.7 %copy-start.5 = (bf16[256,8,128]{2,0,1:T(8,128)(2,1)}, bf16[256,8,128]{2,0,1:T(8,128)(2,1)S(1)}, u32[]{:S(2)}) copy-start(bf16[256,8,128]{2,0,1:T(8,128)(2,1)S(1)} %collective-permute-done.11) | copy-start | bytes 1572868
  149.8 10.1 %all-to-all-start.7 = ((bf16[256,8,128]{2,1,0:T(8,128)(2,1)}), bf16[256,8,128]{2,1,0:T(8,128)(2,1)S(1)}, u32[]{:S(2)}, u32[]{:S(2)}) async-start(bf16[256,8,128]{2,1,0:T(8,128)(2,1)} %copy.65), calls=%async_computation.7 | async-start | bytes 1048576 | tf_op jit(solution)/shard_map/all_to_all | solution.py:110
  (3 other events, 12.7 us)
where the time goes:
time: 162 us; the launch traced here: 161 us
  starting transfers between devices  49.6 us (31%)
  waiting for transfers between devices  38.7 us (24%)
  blocking collectives  22 us (14%)
  local copies, waits for them, and re-layouts  21.2 us (13%)
  matrix products  19.7 us (12%)
  other arithmetic  8.54 us (5%)
    ppermute x12, starting transfers between devices, from_behind(): return lax.ppermute(block, axis, route)  28.6 us
    ppermute x12, waiting for transfers between devices, from_behind(): return lax.ppermute(block, axis, route)  24.2 us
    all_to_all x1, blocking collectives, local(): lax.all_to_all(values, 'head', split_axis=1, concat_axis=0, tiled=True)  11.2 us
    all_to_all x1, blocking collectives, local(): lax.all_to_all(keys, 'head', split_axis=1, concat_axis=0, tiled=True)  10.8 us
    sub x1, matrix products, attend(): weights = jnp.exp(scores - highest)  7.57 us
    unnamed x25, local copies, waits for them, and re-layouts  7.25 us
    all_to_all x1, waiting for transfers between devices, local(): lax.all_to_all(queries, 'head', split_axis=1, concat_axis=0, tiled=True)  5.35 us
    all_to_all x1, waiting for transfers between devices, local(): lax.all_to_all(out_grad, 'head', split_axis=1, concat_axis=0, tiled=True)  4.71 us
  transfers between devices with their start and end apart: 18, of which 6 were waited for; matrix products, arithmetic and copies ran while one was open for 24% of the time, Pallas kernels for 0%

commit v1 on v0

--- a/solution.py
+++ b/solution.py
@@ -5,6 +5,13 @@
 from jax.sharding import PartitionSpec as P
 
 R = 3
+
+
+def exchange_blocks(array, name, split, join):
+    size = lax.axis_size(name)
+    pieces = jnp.stack(jnp.split(array, size, axis=split), axis=0)
+    pieces = lax.all_to_all(pieces, name, split_axis=0, concat_axis=0)
+    return jnp.concatenate(pieces, axis=join)
 
 
 def from_behind(block, axis, distance):
@@ -103,7 +110,7 @@
         value_total = value_total + back_value.astype(jnp.float32)
     return (
         lax.all_to_all(attended, "head", split_axis=0, concat_axis=1, tiled=True),
-        lax.all_to_all(grad_query, "head", split_axis=0, concat_axis=1, tiled=True),
+        exchange_blocks(grad_query, "head", 0, 1),
         lax.all_to_all(
             key_total.astype(jnp.bfloat16), "head", split_axis=0, concat_axis=1, tiled=True
         ),

time: 162 us -> 171 us (1.056)
  waiting for transfers between devices: 38.7 us -> 44.6 us
    ppermute x12, waiting for transfers between devices: 24.2 us -> 29.7 us  [from_behind(): return lax.ppermute(block, axis, route)]
    unnamed x25 -> x34, local copies, waits for them, and re-layouts: 7.25 us -> 10.3 us
    convert_element_type x1 -> x0, local copies, waits for them, and re-layouts: 2.12 us -> none  [attend(): grad_query = (jnp.einsum('hts,shd->thd', grad_scores, key_window, preferr...]
    concatenate x1, local copies, waits for them, and re-layouts: 0.06 us -> 1.89 us  [local(): value_window = jnp.concatenate(value_tiles, axis=0)]
  transfers between devices with their start and end apart: 18 -> 18, of which waited for: 6 -> 7; matrix products, arithmetic and copies ran while one was open for 24% -> 22% of each run, Pallas kernels for 0% -> 0%
where the time goes in v1:
time: 171 us; the launch traced here: 170 us
  starting transfers between devices  49.6 us (29%)
  waiting for transfers between devices  44.6 us (26%)
  local copies, waits for them, and re-layouts  22.4 us (13%)
  blocking collectives  22 us (13%)
  matrix products  21.2 us (12%)
  other arithmetic  9.36 us (5%)
    ppermute x12, waiting for transfers between devices, from_behind(): return lax.ppermute(block, axis, route)  29.7 us
    ppermute x12, starting transfers between devices, from_behind(): return lax.ppermute(block, axis, route)  28.6 us
    all_to_all x1, blocking collectives, local(): lax.all_to_all(values, 'head', split_axis=1, concat_axis=0, tiled=True)  11.2 us
    all_to_all x1, blocking collectives, local(): lax.all_to_all(keys, 'head', split_axis=1, concat_axis=0, tiled=True)  10.8 us
    unnamed x34, local copies, waits for them, and re-layouts  10.3 us
    sub x1, matrix products, attend(): weights = jnp.exp(scores - highest)  7.09 us
    all_to_all x1, waiting for transfers between devices, local(): lax.all_to_all(out_grad, 'head', split_axis=1, concat_axis=0, tiled=True)  5.48 us
    all_to_all x1, waiting for transfers between devices, local(): lax.all_to_all(queries, 'head', split_axis=1, concat_axis=0, tiled=True)  5.35 us
  transfers between devices with their start and end apart: 18, of which 7 were waited for; matrix products, arithmetic and copies ran while one was open for 22% of the time, Pallas kernels for 0%

profile of v1, /device:TPU:10, one launch (start us, length us, event | category | flops | bytes accessed | tf_op | source)
XLA Modules:
  0.0 170.2 jit_solution(16244883051528491758)
XLA Ops:
  1.9 10.8 %all_to_all.131 = bf16[128,16,128]{2,0,1:T(8,128)(2,1)S(1)} all-to-all(bf16[128,16,128]{2,0,1:T(8,128)(2,1)S(1)} %copy.46), channel_id=1, replica_groups=mesh['ctx'=16,'head'=2] {'head'}, dimensions={1} | all-to-all | bytes 1048576 | tf_op jit(solution)/shard_map/all_to_all | solution.py:70
  15.9 11.2 %all_to_all.132 = bf16[128,16,128]{2,0,1:T(8,128)(2,1)S(1)} all-to-all(bf16[128,16,128]{2,0,1:T(8,128)(2,1)S(1)} %copy.44), channel_id=1, replica_groups=mesh['ctx'=16,'head'=2] {'head'}, dimensions={1} | all-to-all | bytes 1048576 | tf_op jit(solution)/shard_map/all_to_all | solution.py:71
  27.8 2.4 %collective-permute-start = (bf16[256,8,128]{0,2,1:T(8,128)(2,1)S(1)}, bf16[256,8,128]{0,2,1:T(8,128)(2,1)}, u32[]{:S(2)}, u32[]{:S(2)}) collective-permute-start(bf16[256,8,128]{0,2,1:T(8,128)(2,1)S(1)} %all_to_all.97), channel_id=1, source_target_pairs={{0,2},{2,4},{4,6},{6,8},{8,10},{10,12},{12,14},{14,16},{16,18},{18... | collective-permute-start | bytes 1572872 | tf_op jit(solution)/shard_map/ppermute | solution.py:20
  30.2 3.2 %collective-permute-start.4 = (bf16[256,8,128]{2,0,1:T(8,128)(2,1)S(1)}, bf16[256,8,128]{2,0,1:T(8,128)(2,1)}, u32[]{:S(2)}, u32[]{:S(2)}) collective-permute-start(bf16[256,8,128]{2,0,1:T(8,128)(2,1)S(1)} %collective-permute-done.3), channel_id=1, source_target_pairs={{0,2},{2,4},{4,6},{6,8},{8,10},{10,12},{12,14},{14,16},{16,18},{18... | collective-permute-start | bytes 1572872 | tf_op jit(solution)/shard_map/ppermute | solution.py:20
  34.3 3.5 %all-to-all-start.2 = ((bf16[128,16,128]{2,0,1:T(8,128)(2,1)}), bf16[128,16,128]{2,0,1:T(8,128)(2,1)S(1)}, u32[]{:S(2)}, u32[]{:S(2)}) async-start(bf16[128,16,128]{2,0,1:T(8,128)(2,1)} %copy.48), calls=%async_computation.2 | async-start | bytes 1048576 | tf_op jit(solution)/shard_map/all_to_all | solution.py:69
  38.9 2.3 %collective-permute-start.1 = (bf16[256,8,128]{0,2,1:T(8,128)(2,1)}, bf16[256,8,128]{0,2,1:T(8,128)(2,1)}, u32[]{:S(2)}, u32[]{:S(2)}) collective-permute-start(bf16[256,8,128]{0,2,1:T(8,128)(2,1)} %collective-permute-done), channel_id=1, source_target_pairs={{0,2},{2,4},{4,6},{6,8},{8,10},{10,12},{12,14},{14,16},{16,18},{18... | collective-permute-start | bytes 1572872 | tf_op jit(solution)/shard_map/ppermute | solution.py:20
  41.3 5.3 %all-to-all-done.2 = bf16[128,16,128]{2,0,1:T(8,128)(2,1)S(1)} async-done(((bf16[128,16,128]{2,0,1:T(8,128)(2,1)}), bf16[128,16,128]{2,0,1:T(8,128)(2,1)S(1)}, u32[]{:S(2)}, u32[]{:S(2)}) %all-to-all-start.2) | async-done | bytes 524320 | tf_op jit(solution)/shard_map/all_to_all | solution.py:69
  46.6 3.5 %all-to-all-start.4 = ((bf16[128,16,128]{2,0,1:T(8,128)(2,1)}), bf16[128,16,128]{2,0,1:T(8,128)(2,1)S(1)}, u32[]{:S(2)}, u32[]{:S(2)}) async-start(bf16[128,16,128]{2,0,1:T(8,128)(2,1)} %copy.53), calls=%async_computation.4 | async-start | bytes 1048576 | tf_op jit(solution)/shard_map/all_to_all | solution.py:72
  52.7 5.5 %all-to-all-done.4 = bf16[128,16,128]{2,0,1:T(8,128)(2,1)S(1)} async-done(((bf16[128,16,128]{2,0,1:T(8,128)(2,1)}), bf16[128,16,128]{2,0,1:T(8,128)(2,1)S(1)}, u32[]{:S(2)}, u32[]{:S(2)}) %all-to-all-start.4) | async-done | bytes 524320 | tf_op jit(solution)/shard_map/all_to_all | solution.py:72
  65.7 7.1 %fusion.23 = (f32[8,256]{1,0:T(8,128)S(1)}, f32[8,256,1024]{1,2,0:T(8,128)}) fusion(pred[256,1024]{0,1:T(8,128)(4,1)S(1)} %fusion.16, bf16[256,8,128]{2,0,1:T(8,128)(2,1)S(1)} %bitcast.93, bf16[256,8,128]{2,0,1:T(8,128)(2,1)} %collective-permute-done.5, bf16[256,8,128]{2,0,1:T(8,128)(2,1)} %collective-permute-done.4, ...), kind=kOutput, calls=%fused_computation.50 | convolution fusion | flops 553649152 | bytes 11280384 | tf_op jit(solution)/shard_map/sub | solution.py:31
  72.7 4.3 %fusion.6 = bf16[8,256,1024]{1,2,0:T(8,128)(2,1)S(1)} fusion(f32[8,256,1024]{1,2,0:T(8,128)} %get-tuple-element.25, f32[8,256]{1,0:T(8,128)S(1)} %get-tuple-element.24), kind=kLoop, calls=%fused_computation.11 | loop fusion | flops 4194304 | bytes 12591104 | tf_op jit(solution)/shard_map/convert_element_type | solution.py:33
  77.0 3.3 %fusion.25 = (bf16[1024,8,128]{2,0,1:T(8,128)(2,1)S(1)}, f32[1024,8,128]{2,0,1:T(8,128)}) fusion(bf16[8,256,1024]{1,2,0:T(8,128)(2,1)S(1)} %fusion.6, bf16[256,8,128]{0,2,1:T(8,128)(2,1)S(1)} %all_to_all.113), kind=kOutput, calls=%fused_computation.52 | convolution fusion | flops 537919488 | bytes 11010048 | tf_op jit(solution)/shard_map/hts,thd->shd/dot_general | solution.py:52
  82.2 2.3 %multiply_reduce_fusion = (f32[256,8]{0,1:T(8,128)S(1)}, bf16[256,8,128]{0,2,1:T(8,128)(2,1)S(1)}) fusion(bf16[256,8,128]{0,2,1:T(8,128)(2,1)S(1)} %all_to_all.113, bf16[1024,8,128]{0,2,1:T(8,128)(2,1)} %constant_dynamic-update-slice_fusion, bf16[8,256,1024]{1,2,0:T(8,128)(2,1)S(1)} %fusion.6), kind=kOutput, calls=%fused_computation.27 | convolution fusion | flops 538179584 | bytes 7348224 | tf_op jit(solution)/shard_map/hts,shd->thd/dot_general | solution.py:34
  84.6 3.2 %fusion.1 = bf16[8,256,1024]{1,2,0:T(8,128)(2,1)S(1)} fusion(f32[8,256]{1,0:T(8,128)S(1)} %bitcast.101, f32[8,256,1024]{1,2,0:T(8,128)S(1)} %bitcast.82, f32[8,256]{1,0:T(8,128)S(1)} %get-tuple-element.24, bf16[1024,8,128]{0,2,1:T(8,128)(2,1)} %constant_dynamic-update-slice_fusion, bf16[256,8,128]{0,2,1:T(8,128)(2,1)S(1)} %all_to_all.113), kind=kOutput, calls=%fused_computation.2 | convolution fusion | flops 545259520 | bytes 15220736 | tf_op jit(solution)/shard_map/thd,shd->hts/dot_general | solution.py:37
  87.8 3.2 %fusion.24 = (bf16[1024,8,128]{2,0,1:T(8,128)(2,1)S(1)}, f32[1024,8,128]{2,0,1:T(8,128)}) fusion(bf16[8,256,1024]{1,2,0:T(8,128)(2,1)S(1)} %fusion.1, bf16[256,8,128]{2,0,1:T(8,128)(2,1)S(1)} %bitcast.94), kind=kOutput, calls=%fused_computation.51 | convolution fusion | flops 538968064 | bytes 11010048 | tf_op jit(solution)/shard_map/hts,thd->shd/dot_general | solution.py:49
  92.2 3.8 %collective-permute-start.6 = (bf16[256,8,128]{2,0,1:T(8,128)(2,1)}, bf16[256,8,128]{2,0,1:T(8,128)(2,1)}, u32[]{:S(2)}, u32[]{:S(2)}) collective-permute-start(bf16[256,8,128]{2,0,1:T(8,128)(2,1)} %get-tuple-element.19), channel_id=1, source_target_pairs={{2,0},{4,2},{6,4},{8,6},{10,8},{12,10},{14,12},{16,14},{18,16},{20... | collective-permute-start | bytes 1572872 | tf_op jit(solution)/shard_map/ppermute | solution.py:20
  100.2 3.4 %collective-permute-start.7 = (bf16[256,8,128]{2,0,1:T(8,128)(2,1)}, bf16[256,8,128]{2,0,1:T(8,128)(2,1)}, u32[]{:S(2)}, u32[]{:S(2)}) collective-permute-start(bf16[256,8,128]{2,0,1:T(8,128)(2,1)} %get-tuple-element.21), channel_id=1, source_target_pairs={{4,0},{6,2},{8,4},{10,6},{12,8},{14,10},{16,12},{18,14},{20,16},{2... | collective-permute-start | bytes 1572872 | tf_op jit(solution)/shard_map/ppermute | solution.py:20
  104.4 3.5 %all-to-all-start.5 = ((bf16[2,128,8,128]{1,3,2,0:T(8,128)(2,1)}), bf16[2,128,8,128]{1,3,2,0:T(8,128)(2,1)S(1)}, u32[]{:S(2)}, u32[]{:S(2)}) async-start(bf16[2,128,8,128]{1,3,2,0:T(8,128)(2,1)} %pad_maximum_fusion.1), calls=%async_computation.5 | async-start | bytes 1048576 | tf_op jit(solution)/shard_map/all_to_all | solution.py:13
  116.6 3.5 %all-to-all-start.3 = ((bf16[256,8,128]{2,1,0:T(8,128)(2,1)}), bf16[256,8,128]{2,1,0:T(8,128)(2,1)S(1)}, u32[]{:S(2)}, u32[]{:S(2)}) async-start(bf16[256,8,128]{2,1,0:T(8,128)(2,1)} %copy.51), calls=%async_computation.3 | async-start | bytes 1048576 | tf_op jit(solution)/shard_map/all_to_all | solution.py:112
  120.1 9.5 %collective-permute-done.7 = bf16[256,8,128]{2,0,1:T(8,128)(2,1)} collective-permute-done((bf16[256,8,128]{2,0,1:T(8,128)(2,1)}, bf16[256,8,128]{2,0,1:T(8,128)(2,1)}, u32[]{:S(2)}, u32[]{:S(2)}) %collective-permute-start.7) | collective-permute-done | bytes 524320 | tf_op jit(solution)/shard_map/ppermute | solution.py:20
  132.6 3.5 %all-to-all-start.6 = ((bf16[256,8,128]{2,1,0:T(8,128)(2,1)}), bf16[256,8,128]{2,1,0:T(8,128)(2,1)S(1)}, u32[]{:S(2)}, u32[]{:S(2)}) async-start(bf16[256,8,128]{2,1,0:T(8,128)(2,1)} %copy.59), calls=%async_computation.6 | async-start | bytes 1048576 | tf_op jit(solution)/shard_map/all_to_all | solution.py:114
  138.0 18.3 %collective-permute-done.10 = bf16[256,8,128]{2,0,1:T(8,128)(2,1)} collective-permute-done((bf16[256,8,128]{2,0,1:T(8,128)(2,1)}, bf16[256,8,128]{2,0,1:T(8,128)(2,1)}, u32[]{:S(2)}, u32[]{:S(2)}) %collective-permute-start.10) | collective-permute-done | bytes 524320 | tf_op jit(solution)/shard_map/ppermute | solution.py:20
  159.2 3.5 %all-to-all-start.7 = ((bf16[256,8,128]{2,1,0:T(8,128)(2,1)}), bf16[256,8,128]{2,1,0:T(8,128)(2,1)S(1)}, u32[]{:S(2)}, u32[]{:S(2)}) async-start(bf16[256,8,128]{2,1,0:T(8,128)(2,1)} %copy.62), calls=%async_computation.7 | async-start | bytes 1048576 | tf_op jit(solution)/shard_map/all_to_all | solution.py:117
  165.7 3.6 %all-to-all-done.7 = bf16[256,8,128]{2,1,0:T(8,128)(2,1)S(1)} async-done(((bf16[256,8,128]{2,1,0:T(8,128)(2,1)}), bf16[256,8,128]{2,1,0:T(8,128)(2,1)S(1)}, u32[]{:S(2)}, u32[]{:S(2)}) %all-to-all-start.7) | async-done | bytes 524320 | tf_op jit(solution)/shard_map/all_to_all | solution.py:117
  (85 shorter events, 45.6 us)
Async XLA Ops:
  0.6 32.7 %copy-start.2 = (bf16[128,16,128]{2,1,0:T(8,128)(2,1)S(1)}, bf16[128,16,128]{2,1,0:T(8,128)(2,1)}, u32[]{:S(2)}) copy-start(bf16[128,16,128]{2,1,0:T(8,128)(2,1)} %param.5) | copy-start | bytes 1572868
  1.9 35.9 %copy-start.3 = (bf16[128,16,128]{2,1,0:T(8,128)(2,1)S(1)}, bf16[128,16,128]{2,1,0:T(8,128)(2,1)}, u32[]{:S(2)}) copy-start(bf16[128,16,128]{2,1,0:T(8,128)(2,1)} %param.8) | copy-start | bytes 1572868
  12.7 26.1 %copy-start.10 = (s32[1,3]{1,0:T(1,128)S(1)}, s32[1,3]{1,0:T(1,128)}, u32[]{:S(2)}) copy-start(s32[1,3]{1,0:T(1,128)} %param.9) | copy-start | bytes 40
  12.7 52.9 %copy-start.4 = (bf16[128,2,8,128]{3,0,1,2:T(8,128)(2,1)}, bf16[128,2,8,128]{3,0,1,2:T(8,128)(2,1)S(1)}, u32[]{:S(2)}) copy-start(bf16[128,2,8,128]{3,0,1,2:T(8,128)(2,1)S(1)} %copy.47) | copy-start | bytes 1572868
  12.7 17.4 %collective-permute-start.3 = (bf16[256,8,128]{2,0,1:T(8,128)(2,1)S(1)}, bf16[256,8,128]{2,0,1:T(8,128)(2,1)S(1)}, u32[]{:S(2)}, u32[]{:S(2)}) collective-permute-start(bf16[256,8,128]{2,0,1:T(8,128)(2,1)S(1)} %bitcast.95), channel_id=1, source_target_pairs={{0,2},{2,4},{4,6},{6,8},{8,10},{10,12},{12,14},{14,16},{16,18},{18... | collective-permute-start | bytes 1572872 | tf_op jit(solution)/shard_map/ppermute | solution.py:20
  27.8 11.2 %collective-permute-start = (bf16[256,8,128]{0,2,1:T(8,128)(2,1)S(1)}, bf16[256,8,128]{0,2,1:T(8,128)(2,1)}, u32[]{:S(2)}, u32[]{:S(2)}) collective-permute-start(bf16[256,8,128]{0,2,1:T(8,128)(2,1)S(1)} %all_to_all.97), channel_id=1, source_target_pairs={{0,2},{2,4},{4,6},{6,8},{8,10},{10,12},{12,14},{14,16},{16,18},{18... | collective-permute-start | bytes 1572872 | tf_op jit(solution)/shard_map/ppermute | solution.py:20
  30.2 28.4 %copy-start.7 = (bf16[256,8,128]{2,0,1:T(8,128)(2,1)}, bf16[256,8,128]{2,0,1:T(8,128)(2,1)S(1)}, u32[]{:S(2)}) copy-start(bf16[256,8,128]{2,0,1:T(8,128)(2,1)S(1)} %collective-permute-done.3) | copy-start | bytes 1572868
  30.2 19.9 %collective-permute-start.4 = (bf16[256,8,128]{2,0,1:T(8,128)(2,1)S(1)}, bf16[256,8,128]{2,0,1:T(8,128)(2,1)}, u32[]{:S(2)}, u32[]{:S(2)}) collective-permute-start(bf16[256,8,128]{2,0,1:T(8,128)(2,1)S(1)} %collective-permute-done.3), channel_id=1, source_target_pairs={{0,2},{2,4},{4,6},{6,8},{8,10},{10,12},{12,14},{14,16},{16,18},{18... | collective-permute-start | bytes 1572872 | tf_op jit(solution)/shard_map/ppermute | solution.py:20
  34.3 12.3 %all-to-all-start.2 = ((bf16[128,16,128]{2,0,1:T(8,128)(2,1)}), bf16[128,16,128]{2,0,1:T(8,128)(2,1)S(1)}, u32[]{:S(2)}, u32[]{:S(2)}) async-start(bf16[128,16,128]{2,0,1:T(8,128)(2,1)} %copy.48), calls=%async_computation.2 | async-start | bytes 1048576 | tf_op jit(solution)/shard_map/all_to_all | solution.py:69
  38.9 22.8 %collective-permute-start.1 = (bf16[256,8,128]{0,2,1:T(8,128)(2,1)}, bf16[256,8,128]{0,2,1:T(8,128)(2,1)}, u32[]{:S(2)}, u32[]{:S(2)}) collective-permute-start(bf16[256,8,128]{0,2,1:T(8,128)(2,1)} %collective-permute-done), channel_id=1, source_target_pairs={{0,2},{2,4},{4,6},{6,8},{8,10},{10,12},{12,14},{14,16},{16,18},{18... | collective-permute-start | bytes 1572872 | tf_op jit(solution)/shard_map/ppermute | solution.py:20
  46.6 11.6 %all-to-all-start.4 = ((bf16[128,16,128]{2,0,1:T(8,128)(2,1)}), bf16[128,16,128]{2,0,1:T(8,128)(2,1)S(1)}, u32[]{:S(2)}, u32[]{:S(2)}) async-start(bf16[128,16,128]{2,0,1:T(8,128)(2,1)} %copy.53), calls=%async_computation.4 | async-start | bytes 1048576 | tf_op jit(solution)/shard_map/all_to_all | solution.py:72
  50.1 15.5 %collective-permute-start.5 = (bf16[256,8,128]{2,0,1:T(8,128)(2,1)}, bf16[256,8,128]{2,0,1:T(8,128)(2,1)}, u32[]{:S(2)}, u32[]{:S(2)}) collective-permute-start(bf16[256,8,128]{2,0,1:T(8,128)(2,1)} %collective-permute-done.4), channel_id=1, source_target_pairs={{0,2},{2,4},{4,6},{6,8},{8,10},{10,12},{12,14},{14,16},{16,18},{18... | collective-permute-start | bytes 1572872 | tf_op jit(solution)/shard_map/ppermute | solution.py:20
  52.7 20.1 %copy-start = (bf16[128,2,8,128]{3,0,1,2:T(8,128)(2,1)}, bf16[128,2,8,128]{3,0,1,2:T(8,128)(2,1)S(1)}, u32[]{:S(2)}) copy-start(bf16[128,2,8,128]{3,0,1,2:T(8,128)(2,1)S(1)} %copy.49) | copy-start | bytes 1572868
  61.8 18.5 %collective-permute-start.2 = (bf16[256,8,128]{0,2,1:T(8,128)(2,1)}, bf16[256,8,128]{0,2,1:T(8,128)(2,1)}, u32[]{:S(2)}, u32[]{:S(2)}) collective-permute-start(bf16[256,8,128]{0,2,1:T(8,128)(2,1)} %collective-permute-done.1), channel_id=1, source_target_pairs={{0,2},{2,4},{4,6},{6,8},{8,10},{10,12},{12,14},{14,16},{16,18},{18... | collective-permute-start | bytes 1572872 | tf_op jit(solution)/shard_map/ppermute | solution.py:20
  92.2 20.9 %collective-permute-start.6 = (bf16[256,8,128]{2,0,1:T(8,128)(2,1)}, bf16[256,8,128]{2,0,1:T(8,128)(2,1)}, u32[]{:S(2)}, u32[]{:S(2)}) collective-permute-start(bf16[256,8,128]{2,0,1:T(8,128)(2,1)} %get-tuple-element.19), channel_id=1, source_target_pairs={{2,0},{4,2},{6,4},{8,6},{10,8},{12,10},{14,12},{16,14},{18,16},{20... | collective-permute-start | bytes 1572872 | tf_op jit(solution)/shard_map/ppermute | solution.py:20
  98.3 21.8 %collective-permute-start.8 = (bf16[256,8,128]{2,0,1:T(8,128)(2,1)}, bf16[256,8,128]{2,0,1:T(8,128)(2,1)}, u32[]{:S(2)}, u32[]{:S(2)}) collective-permute-start(bf16[256,8,128]{2,0,1:T(8,128)(2,1)} %get-tuple-element.20), channel_id=1, source_target_pairs={{6,0},{8,2},{10,4},{12,6},{14,8},{16,10},{18,12},{20,14},{22,16},{... | collective-permute-start | bytes 1572872 | tf_op jit(solution)/shard_map/ppermute | solution.py:20
  100.2 29.4 %collective-permute-start.7 = (bf16[256,8,128]{2,0,1:T(8,128)(2,1)}, bf16[256,8,128]{2,0,1:T(8,128)(2,1)}, u32[]{:S(2)}, u32[]{:S(2)}) collective-permute-start(bf16[256,8,128]{2,0,1:T(8,128)(2,1)} %get-tuple-element.21), channel_id=1, source_target_pairs={{4,0},{6,2},{8,4},{10,6},{12,8},{14,10},{16,12},{18,14},{20,16},{2... | collective-permute-start | bytes 1572872 | tf_op jit(solution)/shard_map/ppermute | solution.py:20
  104.4 12.1 %all-to-all-start.5 = ((bf16[2,128,8,128]{1,3,2,0:T(8,128)(2,1)}), bf16[2,128,8,128]{1,3,2,0:T(8,128)(2,1)S(1)}, u32[]{:S(2)}, u32[]{:S(2)}) async-start(bf16[2,128,8,128]{1,3,2,0:T(8,128)(2,1)} %pad_maximum_fusion.1), calls=%async_computation.5 | async-start | bytes 1048576 | tf_op jit(solution)/shard_map/all_to_all | solution.py:13
  109.1 27.0 %collective-permute-start.9 = (bf16[256,8,128]{2,0,1:T(8,128)(2,1)}, bf16[256,8,128]{2,0,1:T(8,128)(2,1)S(1)}, u32[]{:S(2)}, u32[]{:S(2)}) collective-permute-start(bf16[256,8,128]{2,0,1:T(8,128)(2,1)} %get-tuple-element.16), channel_id=1, source_target_pairs={{2,0},{4,2},{6,4},{8,6},{10,8},{12,10},{14,12},{16,14},{18,16},{20... | collective-permute-start | bytes 1572872 | tf_op jit(solution)/shard_map/ppermute | solution.py:20
  111.2 26.9 %collective-permute-start.11 = (bf16[256,8,128]{2,0,1:T(8,128)(2,1)}, bf16[256,8,128]{2,0,1:T(8,128)(2,1)S(1)}, u32[]{:S(2)}, u32[]{:S(2)}) collective-permute-start(bf16[256,8,128]{2,0,1:T(8,128)(2,1)} %get-tuple-element.17), channel_id=1, source_target_pairs={{6,0},{8,2},{10,4},{12,6},{14,8},{16,10},{18,12},{20,14},{22,16},{... | collective-permute-start | bytes 1572872 | tf_op jit(solution)/shard_map/ppermute | solution.py:20
  113.1 43.2 %collective-permute-start.10 = (bf16[256,8,128]{2,0,1:T(8,128)(2,1)}, bf16[256,8,128]{2,0,1:T(8,128)(2,1)}, u32[]{:S(2)}, u32[]{:S(2)}) collective-permute-start(bf16[256,8,128]{2,0,1:T(8,128)(2,1)} %get-tuple-element.18), channel_id=1, source_target_pairs={{4,0},{6,2},{8,4},{10,6},{12,8},{14,10},{16,12},{18,14},{20,16},{2... | collective-permute-start | bytes 1572872 | tf_op jit(solution)/shard_map/ppermute | solution.py:20
  116.6 16.1 %all-to-all-start.3 = ((bf16[256,8,128]{2,1,0:T(8,128)(2,1)}), bf16[256,8,128]{2,1,0:T(8,128)(2,1)S(1)}, u32[]{:S(2)}, u32[]{:S(2)}) async-start(bf16[256,8,128]{2,1,0:T(8,128)(2,1)} %copy.51), calls=%async_computation.3 | async-start | bytes 1048576 | tf_op jit(solution)/shard_map/all_to_all | solution.py:112
  132.6 26.6 %all-to-all-start.6 = ((bf16[256,8,128]{2,1,0:T(8,128)(2,1)}), bf16[256,8,128]{2,1,0:T(8,128)(2,1)S(1)}, u32[]{:S(2)}, u32[]{:S(2)}) async-start(bf16[256,8,128]{2,1,0:T(8,128)(2,1)} %copy.59), calls=%async_computation.6 | async-start | bytes 1048576 | tf_op jit(solution)/shard_map/all_to_all | solution.py:114
  159.2 10.1 %all-to-all-start.7 = ((bf16[256,8,128]{2,1,0:T(8,128)(2,1)}), bf16[256,8,128]{2,1,0:T(8,128)(2,1)S(1)}, u32[]{:S(2)}, u32[]{:S(2)}) async-start(bf16[256,8,128]{2,1,0:T(8,128)(2,1)} %copy.62), calls=%async_computation.7 | async-start | bytes 1048576 | tf_op jit(solution)/shard_map/all_to_all | solution.py:117
  (7 other events, 64.3 us)
